TPU v7x, 32 devices: a whole 2x2x4 slice. The times are simulated.
32 devices in a mesh: grp: 2 (over x), lat: 16 (over z, y, core).
Axes of the slice: x: 2, y: 2, z: 4, core: 2. Of those that a mesh axis runs over, the one named last changes fastest.
Arguments:
- features: bfloat16 [2, 32, 192, 512], P('grp', 'lat'), parts along dimension 0, may hold values from -120 to 120
- noise_index: int32 [2], P('grp'), parts along dimension 0, may hold values from 0 to 17
- sigma_table: float32 [18], replicated, may hold values from 0.002 to 80
- affine_weight: bfloat16 [128, 1024], replicated, may hold values from -0.5 to 0.5
- norm_gain: float32 [3, 512], replicated, may hold values from 0.1 to 1.9
- norm_bias: float32 [3, 512], replicated, may hold values from -3 to 3
- conv1_weight: bfloat16 [3, 3, 512, 512], replicated, may hold values from -0.09375 to 0.09375
- conv2_weight: bfloat16 [3, 3, 512, 512], replicated, may hold values from -0.09375 to 0.09375
- conv_bias: float32 [2, 512], replicated, may hold values from -3 to 3
- qkv_weight: bfloat16 [512, 1536], replicated, may hold values from -3 to 3
- proj_weight: bfloat16 [512, 512], replicated, may hold values from -0.25 to 0.25
- proj_bias: float32 [512], replicated, may hold values from -3 to 3
Outputs:
- bottleneck: bfloat16 [2, 16, 96, 512], P('grp', 'lat'), parts along dimension 0
There are 2 independent parts, one for each index of `grp`. A program takes and returns all parts, laid end to end along the dimension named above; an argument that names none is the same for every part. Nothing has to cross between parts.
All inputs are finite; a program needn't handle non-finite values.
Results may differ from a plain program's by a relative error of at most 0.012.
The roundings to bfloat16 on the way count: a program that leaves them out, or rounds other values in their place, can miss the bound.
Values may be sent and summed in bfloat16 or wider, within the bound.
A program may use at most 128 MiB of HBM per device.

v0:
```python
import math

import jax
import jax.numpy as jnp
from jax import lax
from jax.sharding import PartitionSpec as P

HEAD_DIM = 64
GROUPS = 32
FREQS = 64


eps = 1e-05
skip_gain = 0.7071067811865476


def with_halo(block, sides, width):
    for axis, dim in sides:
        count = lax.axis_size(axis)
        forward = [(i, i + 1) for i in range(count - 1)]
        backward = [(target, source) for source, target in forward]
        low = lax.ppermute(
            lax.slice_in_dim(block, block.shape[dim] - width, None, axis=dim), axis, forward
        )
        high = lax.ppermute(lax.slice_in_dim(block, 0, width, axis=dim), axis, backward)
        block = jnp.concatenate([low, block, high], axis=dim)
    return block


def noise_terms(noise_index, sigma_table, affine_weight):
    levels_count = sigma_table.shape[0]
    chosen = (noise_index[:, None] == jnp.arange(levels_count, dtype=jnp.int32)[None, :]).astype(
        jnp.float32
    )
    sigmas = jnp.sum(chosen * sigma_table[None, :], axis=1)
    log_level = jnp.log(sigmas) / 4.0
    frequency = jnp.exp(-math.log(10000.0) * jnp.arange(FREQS, dtype=jnp.float32) / FREQS)
    angles = log_level[:, None] * frequency[None, :]
    fourier = jnp.concatenate([jnp.cos(angles), jnp.sin(angles)], axis=1).astype(jnp.bfloat16)
    affine = jnp.dot(fourier, affine_weight, preferred_element_type=jnp.float32)
    channels = affine.shape[1] // 2
    return (affine[:, :channels], affine[:, channels:])


def band_moments(values):
    members, height, breadth, channels = values.shape
    group_width = channels // GROUPS
    entries = height * breadth * group_width * lax.axis_size("lat")
    column_sums = jnp.sum(values, axis=(1, 2)).reshape(members, GROUPS, group_width).sum(axis=2)
    column_squares = (
        jnp.sum(jnp.square(values), axis=(1, 2)).reshape(members, GROUPS, group_width).sum(axis=2)
    )
    totals, squares = lax.psum((column_sums, column_squares), "lat")
    center = totals / entries
    spread = squares / entries - center * center
    return (center, spread)


def normalize(values, center, spread, norm_scale, norm_offset):
    group_width = values.shape[-1] // GROUPS
    center_full = jnp.repeat(center, group_width, axis=1)[:, None, None, :]
    factor_full = jnp.repeat(lax.rsqrt(spread + eps), group_width, axis=1)[:, None, None, :]
    return (values - center_full) * factor_full * norm_scale + norm_offset


def convolve(values, kernel):
    return lax.conv_general_dilated(
        values,
        kernel,
        (1, 1),
        ((0, 0), (1, 1)),
        dimension_numbers=("NHWC", "HWIO", "NHWC"),
        preferred_element_type=jnp.float32,
    )


def with_rims(values):
    return with_halo(values, (("lat", 1),), 1)


def key_span(total_rows, breadth):
    row_limit = max(1, 1024 // breadth)
    return math.gcd(total_rows, 1 << row_limit.bit_length() - 1)


def accumulate(running, queries, key_block, value_block):
    blended, largest, totals = running
    scores = jnp.einsum(
        "mqhd,mkhd->mqhk", queries, key_block, preferred_element_type=jnp.float32
    ) * HEAD_DIM ** (-0.5)
    rising = jnp.maximum(largest, jnp.max(scores, axis=-1))
    fading = jnp.exp(largest - rising)
    weights = jnp.exp(scores - rising[..., None])
    totals = totals * fading + jnp.sum(weights, axis=-1)
    blended = blended * fading[..., None] + jnp.einsum(
        "mqhk,mkhd->mqhd",
        weights.astype(jnp.bfloat16),
        value_block,
        preferred_element_type=jnp.float32,
    )
    return (blended, rising, totals)


def local(
    features,
    noise_index,
    sigma_table,
    affine_weight,
    norm_gain,
    norm_bias,
    conv1_weight,
    conv2_weight,
    conv_bias,
    qkv_weight,
    proj_weight,
    proj_bias,
):
    film_scale, film_shift = noise_terms(noise_index, sigma_table, affine_weight)
    film_scale = film_scale[:, None, None, :]
    film_shift = film_shift[:, None, None, :]
    source = features.astype(jnp.float32)
    center, spread = band_moments(source)
    active = jax.nn.silu(normalize(source, center, spread, norm_gain[0], norm_bias[0])).astype(
        jnp.bfloat16
    )
    first_conv = convolve(with_rims(active), conv1_weight) + conv_bias[0]
    center, spread = band_moments(first_conv)
    middle = jax.nn.silu(
        normalize(first_conv, center, spread, norm_gain[1], norm_bias[1]) * (1.0 + film_scale)
        + film_shift
    ).astype(jnp.bfloat16)
    second_conv = convolve(with_rims(middle), conv2_weight)
    level_one = ((source + second_conv + conv_bias[1]) * skip_gain).astype(jnp.bfloat16)
    level_one = lax.optimization_barrier(level_one)
    members, height, breadth, channels = level_one.shape
    low_rows = height // 2
    breadth_low = breadth // 2
    pooled = jnp.mean(
        level_one.astype(jnp.float32).reshape(members, low_rows, 2, breadth_low, 2, channels),
        axis=(2, 4),
    )
    center, spread = band_moments(pooled)
    normed = normalize(pooled, center, spread, norm_gain[2], norm_bias[2]).astype(jnp.bfloat16)
    tokens = low_rows * breadth_low
    head_count = channels // HEAD_DIM
    flat_rows = normed.reshape(members * tokens, channels)
    all_rows = low_rows * lax.axis_size("lat")
    span_rows = key_span(all_rows, breadth_low)
    span_count = all_rows // span_rows
    running = (
        jnp.zeros((members, tokens, head_count, HEAD_DIM), jnp.float32),
        jnp.full((members, tokens, head_count), -1e30, jnp.float32),
        jnp.zeros((members, tokens, head_count), jnp.float32),
    )
    projected = jnp.dot(flat_rows, qkv_weight, preferred_element_type=jnp.float32).astype(
        jnp.bfloat16
    )
    projected = projected.reshape(members, low_rows, breadth_low, 3, channels)
    queries = projected[:, :, :, 0].reshape(members, tokens, head_count, HEAD_DIM)
    key_all, value_all = (
        lax.all_gather(projected[:, :, :, 1], "lat", axis=1, tiled=True),
        lax.all_gather(projected[:, :, :, 2], "lat", axis=1, tiled=True),
    )

    def key_span_step(step_index, inner_state):
        key_slab = lax.dynamic_slice_in_dim(key_all, step_index * span_rows, span_rows, 1).reshape(
            members, span_rows * breadth_low, head_count, HEAD_DIM
        )
        value_slab = lax.dynamic_slice_in_dim(
            value_all, step_index * span_rows, span_rows, 1
        ).reshape(members, span_rows * breadth_low, head_count, HEAD_DIM)
        return accumulate(inner_state, queries, key_slab, value_slab)

    running = lax.fori_loop(0, span_count, key_span_step, running)
    blended, largest, totals = running
    attended = (
        (blended / totals[..., None]).reshape(members * tokens, channels).astype(jnp.bfloat16)
    )
    output_proj = jnp.dot(attended, proj_weight, preferred_element_type=jnp.float32) + proj_bias
    return ((pooled + output_proj.reshape(pooled.shape)) * skip_gain).astype(jnp.bfloat16)


def solution(mesh):
    return jax.shard_map(
        local,
        mesh=mesh,
        in_specs=(
            P("grp", "lat", None, None),
            P("grp"),
            P(),
            P(),
            P(),
            P(),
            P(),
            P(),
            P(),
            P(),
            P(),
            P(),
        ),
        out_specs=P("grp", "lat", None, None),
        check_vma=False,
    )
```

profile of v0, /device:TPU:0, one launch (start us, length us, event | category | flops | bytes accessed | tf_op | source)
XLA Modules:
  0.0 249.0 jit_solution(6614196855762687472)
XLA Ops:
  6.5 1.2 convert_reduce_fusion
  7.8 0.8 fusion.72
  8.6 0.8 fusion.73
  9.8 34.9 %all-reduce.2 = (f32[1,32]{1,0:T(1,128)S(1)}, f32[1,32]{1,0:T(1,128)S(1)}) all-reduce(f32[1,32]{1,0:T(1,128)S(1)} %bitcast.170, f32[1,32]{1,0:T(1,128)S(1)} %bitcast.168), channel_id=1, replica_groups=mesh['grp'=2,'lat'=16] {'lat'}, use_global_device_ids=true, to_apply=%region_5.0 | all-reduce | flops 64 | bytes 512 | tf_op jit(solution)/shard_map/psum | solution.py:53
  45.1 1.3 fusion.45
  46.4 1.3 collective-permute-start
  47.7 1.3 collective-permute-start.1
  49.6 1.3 fusion.57
  51.8 0.8 fusion.74
  52.5 1.1 fusion.58
  55.0 1.2 copy-done.7
  56.2 2.2 select_reduce_fusion.1
  58.7 30.7 %all-reduce.1 = (f32[1,32]{1,0:T(1,128)S(1)}, f32[1,32]{1,0:T(1,128)S(1)}) all-reduce(f32[1,32]{1,0:T(1,128)S(1)} %bitcast.171, f32[1,32]{1,0:T(1,128)S(1)} %bitcast.167), channel_id=1, replica_groups=mesh['grp'=2,'lat'=16] {'lat'}, use_global_device_ids=true, to_apply=%region_11.12 | all-reduce | flops 64 | bytes 512 | tf_op jit(solution)/shard_map/psum | solution.py:53
  90.6 1.3 collective-permute-start.2
  92.6 1.5 collective-permute-start.3
  94.7 1.5 collective-permute-done.3
  96.2 1.3 maximum_bitcast_fusion.1
  98.0 4.4 %convolution_select_fusion = f32[2,8,25,512]{3,1,2,0:T(8,128)S(1)} fusion(bf16[3,3,512,512]{3,2,1,0:T(8,128)(2,1)} %param.21, bf16[4,1,7,2,512]{4,2,3,0,1:T(8,128)(2,1)S(1)} %slice.92, bf16[4,1,8,25,512]{4,2,3,0,1:T(8,128)(2,1)S(1)} %copy.102, pred[8,25]{0,1:T(8,128)(4,1)S(1)} %copy-done.8), kind=kOutput, calls=%fused_computation.30 | convolution fusion | flops 1890295808 | bytes 6414536 | tf_op jit(solution)/shard_map/conv_general_dilated | solution.py:67
  104.9 34.2 %all-reduce = (f32[1,32]{1,0:T(1,128)S(1)}, f32[1,32]{1,0:T(1,128)S(1)}) all-reduce(f32[1,32]{1,0:T(1,128)S(1)} %bitcast.169, f32[1,32]{1,0:T(1,128)S(1)} %bitcast.166), channel_id=1, replica_groups=mesh['grp'=2,'lat'=16] {'lat'}, use_global_device_ids=true, to_apply=%region_20.21 | all-reduce | flops 64 | bytes 512 | tf_op jit(solution)/shard_map/psum | solution.py:53
  142.1 36.1 %all-gather.7.cloned.1.call-done = bf16[1,16,96,1,512]{4,2,3,0,1:T(8,128)(2,1)} async-done(((bf16[1,1,96,1,512]{4,2,3,0,1:T(8,128)(2,1)}), bf16[1,16,96,1,512]{4,2,3,0,1:T(8,128)(2,1)}) %all-gather.7.cloned.1.call-update) | async-done | bytes 1572880 | tf_op jit(solution)/shard_map/all_gather | solution.py:162
  178.2 40.9 %all-gather.5.cloned.1.call-done = bf16[1,16,96,1,512]{4,2,3,0,1:T(8,128)(2,1)} async-done(((bf16[1,1,96,1,512]{4,2,3,0,1:T(8,128)(2,1)}), bf16[1,16,96,1,512]{4,2,3,0,1:T(8,128)(2,1)}) %all-gather.5.cloned.1.call-update) | async-done | bytes 1572880 | tf_op jit(solution)/shard_map/all_gather | solution.py:161
  219.1 20.1 %while.18 = (s32[]{:T(128)}, f32[1,96,8,64]{1,3,2,0:T(8,128)}, f32[1,96,8]{1,2,0:T(8,128)S(1)}, f32[1,96,8]{1,2,0:T(8,128)S(1)}, bf16[1,16,96,512]{3,2,1,0:T(8,1...) while((s32[]{:T(128)}, f32[1,96,8,64]{1,3,2,0:T(8,128)}, ...), condition=%wide.region_24.25_spmd.clone, body=%wide.region_21.24_spmd.clone.sunk | while | flops 155865600 | bytes 23347460 | solution.py:174
  219.1 2.4 constant_dynamic-slice_fusion.3
  221.5 1.7 copy.121
  223.2 1.8 reshape.314
  225.7 0.9 reshape.315
  229.2 2.4 constant_dynamic-slice_fusion.3
  231.6 1.7 copy.121
  233.3 1.8 reshape.314
  235.8 0.9 reshape.315
  239.2 1.0 divide_convert_fusion
  240.2 2.0 fusion.24
  (109 shorter events, 17.0 us)
Async XLA Ops:
  6.5 132.9 %copy-start = (bf16[512,1536]{1,0:T(8,128)(2,1)S(1)}, bf16[512,1536]{1,0:T(8,128)(2,1)}, u32[]{:S(2)}) copy-start(bf16[512,1536]{1,0:T(8,128)(2,1)} %param.23) | copy-start | bytes 4718596
  6.5 171.7 %all-gather.7.cloned.1.call-start = ((), (), s32[]{:S(2)}) async-start(), calls=%async_computation.1 | async-start | bytes 1671168 | tf_op jit(solution)/shard_map/all_gather | solution.py:162
  46.4 7.3 %collective-permute-start = (bf16[1,1,192,512]{3,2,1,0:T(8,128)(2,1)S(1)}, bf16[1,1,192,512]{3,2,1,0:T(8,128)(2,1)S(1)}, u32[]{:S(2)}, u32[]{:S(2)}) collective-permute-start(bf16[1,1,192,512]{3,2,1,0:T(8,128)(2,1)S(1)} %get-tuple-element.235), channel_id=1, source_target_pairs={{0,1},{1,2},{2,3},{3,4},{4,5},{5,6},{6,7},{7,8},{8,9},{9,10},{10,1... | collective-permute-start | bytes 589832 | tf_op jit(solution)/shard_map/ppermute | solution.py:22
  47.7 6.0 %collective-permute-start.1 = (bf16[1,1,192,512]{3,2,1,0:T(8,128)(2,1)S(1)}, bf16[1,1,192,512]{3,2,1,0:T(8,128)(2,1)S(1)}, u32[]{:S(2)}, u32[]{:S(2)}) collective-permute-start(bf16[1,1,192,512]{3,2,1,0:T(8,128)(2,1)S(1)} %get-tuple-element.236), channel_id=1, source_target_pairs={{1,0},{2,1},{3,2},{4,3},{5,4},{6,5},{7,6},{8,7},{9,8},{10,9},{11,1... | collective-permute-start | bytes 589832 | tf_op jit(solution)/shard_map/ppermute | solution.py:25
  53.8 2.3 copy-start.7
  53.8 2.3 copy-start.8
  90.6 3.7 %collective-permute-start.2 = (bf16[1,1,192,512]{3,2,1,0:T(8,128)(2,1)S(1)}, bf16[1,1,192,512]{3,2,1,0:T(8,128)(2,1)S(1)}, u32[]{:S(2)}, u32[]{:S(2)}) collective-permute-start(bf16[1,1,192,512]{3,2,1,0:T(8,128)(2,1)S(1)} %slice.88), channel_id=1, source_target_pairs={{0,1},{1,2},{2,3},{3,4},{4,5},{5,6},{6,7},{7,8},{8,9},{9,10},{10,1... | collective-permute-start | bytes 589832 | tf_op jit(solution)/shard_map/ppermute | solution.py:22
  92.6 3.6 %collective-permute-start.3 = (bf16[1,1,192,512]{3,1,2,0:T(2,128)(2,1)S(1)}, bf16[1,1,192,512]{3,1,2,0:T(2,128)(2,1)S(1)}, u32[]{:S(2)}, u32[]{:S(2)}) collective-permute-start(bf16[1,1,192,512]{3,1,2,0:T(2,128)(2,1)S(1)} %slice.91), channel_id=1, source_target_pairs={{1,0},{2,1},{3,2},{4,3},{5,4},{6,5},{7,6},{8,7},{9,8},{10,9},{11,1... | collective-permute-start | bytes 589832 | tf_op jit(solution)/shard_map/ppermute | solution.py:25
  102.5 1.0 copy-start.4
  104.4 37.4 %copy-start.5 = (f32[96,512]{1,0:T(8,128)}, f32[96,512]{1,0:T(8,128)S(1)}, u32[]{:S(2)}) copy-start(f32[96,512]{1,0:T(8,128)S(1)} %reduce_sum.173) | copy-start | bytes 589828
  141.1 78.0 %all-gather.5.cloned.1.call-start = ((), (), s32[]{:S(2)}) async-start(), calls=%async_computation | async-start | bytes 1671168 | tf_op jit(solution)/shard_map/all_gather | solution.py:161
  219.1 21.1 %copy-start.6 = (f32[512]{0:T(512)S(1)}, f32[512]{0:T(512)}, u32[]{:S(2)}) copy-start(f32[512]{0:T(512)} %param.25) | copy-start | bytes 6148
  226.6 1.1 copy-start.1
  226.6 1.2 copy-start.2
  228.5 0.7 copy-start.3
  236.6 1.1 copy-start.1
  236.6 1.2 copy-start.2
  238.5 0.7 copy-start.3
Sparse Core Ops, SparseCore 0:
  141.3 36.9 all-gather.6
  180.5 38.5 all-gather.4
where the time goes:
time: 250 us; the launch traced here: 249 us
  blocking collectives  99.9 us (40%)
  waiting for transfers between devices  78.6 us (31%)
  local copies, waits for them, and re-layouts  27.8 us (11%)
  between operations  15.2 us (6%)
  matrix products  12.7 us (5%)
  other arithmetic  9.37 us (4%)
  starting transfers between devices  5.41 us (2%)
    psum x3, blocking collectives, band_moments(): totals, squares = lax.psum((column_sums, column_squares), 'lat')  99.9 us
    all_gather x1, waiting for transfers between devices, local(): lax.all_gather(projected[:, :, :, 1], 'lat', axis=1, tiled=True)  40.9 us
    all_gather x1, waiting for transfers between devices, local(): lax.all_gather(projected[:, :, :, 2], 'lat', axis=1, tiled=True)  36.1 us
    dynamic_slice x4, local copies, waits for them, and re-layouts, key_span_step(): lax.dynamic_slice_in_dim(value_all, step_index * span_rows, span_rows, 1)  8.14 us
    conv_general_dilated x2, matrix products, convolve(): lax.conv_general_dilated(values, kernel, (1, 1), ((0, 0), (1, 1)), dimens...  6.59 us
    another operation x4, local copies, waits for them, and re-layouts  5.28 us
  transfers between devices with their start and end apart: 6, of which 3 were waited for; matrix products, arithmetic and copies ran while one was open for 2% of the time, Pallas kernels for 0%

commit v1 on v0

v1 whole, which is shorter than its diff:
```python
import math

import jax
import jax.numpy as jnp
from jax import lax
from jax.experimental import pallas as pl
from jax.experimental.pallas import tpu as pltpu
from jax.sharding import PartitionSpec as P

HEAD_DIM = 64
GROUPS = 32
FREQS = 64
LANES = 128

eps = 1e-05
skip_gain = 0.7071067811865476


def group_totals(sums, group_width):
    lane = lax.broadcasted_iota(jnp.int32, sums.shape, 1)
    step = 1
    while step < group_width:
        ahead = pltpu.roll(sums, LANES - step, 1)
        behind = pltpu.roll(sums, step, 1)
        sums = sums + jnp.where((lane // step) % 2 == 0, ahead, behind)
        step *= 2
    return sums


def silu(values):
    return values / (1.0 + jnp.exp(-values))


def kernel(
    n,
    noise_ref,
    sigma_ref,
    features_ref,
    affine_hbm,
    gain_ref,
    bias_ref,
    conv1_hbm,
    conv2_hbm,
    conv_bias_ref,
    qkv_hbm,
    proj_hbm,
    proj_bias_ref,
    out_ref,
    affine,
    w1,
    w2,
    wqkv,
    wproj,
    abuf,
    first,
    edges,
    halo1,
    halo2,
    stats,
    gath,
    pooled_ref,
    qm,
    top,
    total,
    acc,
    w_sem,
    stat_send,
    stat_recv,
    halo_send,
    halo_recv,
    g_send,
    g_recv,
):
    me = lax.axis_index("lat")
    breadth, channels = features_ref.shape[2], features_ref.shape[3]
    cells = 2 * breadth
    tokens = breadth // 2
    chunks = channels // LANES
    group_width = channels // GROUPS
    planes = n // 4

    loads = []
    for a in range(3):
        for b in range(3):
            loads.append((conv1_hbm.at[a, b], w1.at[b, pl.ds(a * channels, channels)]))
    loads.append((affine_hbm, affine))
    split_at = len(loads)
    for a in range(3):
        for b in range(3):
            loads.append((conv2_hbm.at[a, b], w2.at[b, pl.ds(a * channels, channels)]))
    split_too = len(loads)
    loads.append((qkv_hbm, wqkv))
    loads.append((proj_hbm, wproj))
    loads = [pltpu.make_async_copy(s, d, w_sem.at[i]) for i, (s, d) in enumerate(loads)]
    for load in loads:
        load.start()

    barrier = pltpu.get_barrier_semaphore()

    def greet(j, carry):
        pl.semaphore_signal(
            barrier,
            inc=1,
            device_id={"lat": lax.rem(me + j, n)},
            device_id_type=pl.DeviceIdType.MESH,
        )
        return carry

    lax.fori_loop(1, n, greet, 0)

    def remote(src, dst, send, recv, target):
        return pltpu.make_async_remote_copy(
            src_ref=src,
            dst_ref=dst,
            send_sem=send,
            recv_sem=recv,
            device_id={"lat": target},
            device_id_type=pl.DeviceIdType.MESH,
        )

    def tile_of(sums, squares):
        parts = [sums[:, i * LANES : (i + 1) * LANES] for i in range(chunks)]
        parts += [squares[:, i * LANES : (i + 1) * LANES] for i in range(chunks)]
        return jnp.concatenate(parts, axis=0)

    def share_stats(phase):
        def share(j, carry):
            remote(
                stats.at[phase, 0],
                stats.at[phase, j],
                stat_send.at[phase],
                stat_recv.at[phase],
                lax.rem(me + j, n),
            ).start()
            return carry

        lax.fori_loop(1, n, share, 0)

    def wait_stats(phase, sem):
        others = stats.at[phase, pl.ds(1, n - 1)]
        pltpu.make_async_copy(others, others, sem.at[phase]).wait()

    def moments(phase, entries):
        wait_stats(phase, stat_recv)
        sums = group_totals(jnp.sum(stats[phase], axis=0), group_width)
        center = sums[:chunks] / entries
        spread = sums[chunks:] / entries - center * center
        factor = lax.rsqrt(spread + eps)

        def row(t):
            return jnp.concatenate([t[i : i + 1] for i in range(chunks)], axis=1)

        return row(center), row(factor)

    def halo(phase, src, bufs, act):
        @pl.when(me > 0)
        def _():
            act(
                remote(
                    src(0), bufs.at[1], halo_send.at[phase, 0], halo_recv.at[phase, 1], me - 1
                )
            )

        @pl.when(me < n - 1)
        def _():
            act(
                remote(
                    src(1), bufs.at[0], halo_send.at[phase, 1], halo_recv.at[phase, 0], me + 1
                )
            )

    def halo_arrival(phase, bufs, side):
        pltpu.make_async_copy(bufs.at[side], bufs.at[side], halo_recv.at[phase, side]).wait()

    def store_row(k, values):
        for r in range(2):
            if 0 <= k - r < 3:
                abuf[r, :, (k - r) * channels : (k - r + 1) * channels] = values

    def halo_rows(phase, bufs, formula):
        for side, k, inner in ((0, 0, me > 0), (1, 3, me < n - 1)):

            @pl.when(inner)
            def _():
                halo_arrival(phase, bufs, side)
                store_row(k, formula(bufs[side].astype(jnp.float32)))

            @pl.when(jnp.logical_not(inner))
            def _():
                store_row(k, jnp.zeros((breadth, channels), jnp.bfloat16))

    def convolve(weights):
        lhs = abuf[...].reshape(cells, 3 * channels)
        column = lax.rem(lax.broadcasted_iota(jnp.int32, (cells, channels), 0), breadth)
        low = jnp.dot(lhs, weights[0], preferred_element_type=jnp.float32)
        result = jnp.where(column == 0, 0.0, pltpu.roll(low, 1, 0))
        high = jnp.dot(lhs, weights[2], preferred_element_type=jnp.float32)
        result += jnp.where(column == breadth - 1, 0.0, pltpu.roll(high, cells - 1, 0))
        return result + jnp.dot(lhs, weights[1], preferred_element_type=jnp.float32)

    source = features_ref[0].astype(jnp.float32).reshape(cells, channels)
    stats[0, 0] = tile_of(
        jnp.sum(source, axis=0, keepdims=True), jnp.sum(source * source, axis=0, keepdims=True)
    )
    pl.semaphore_wait(barrier, n - 1)
    share_stats(0)

    def feature_row(r):
        return features_ref.at[0, r]

    halo(0, feature_row, halo1, lambda copy: copy.start())

    sigma = jnp.full((8, 2 * FREQS), sigma_ref[noise_ref[0]], jnp.float32)
    lane = lax.broadcasted_iota(jnp.int32, (8, 2 * FREQS), 1)
    order = lax.rem(lane, FREQS).astype(jnp.float32)
    angles = (jnp.log(sigma) / 4.0) * jnp.exp(-math.log(10000.0) * order / FREQS)
    fourier = jnp.where(lane < FREQS, jnp.cos(angles), jnp.sin(angles)).astype(jnp.bfloat16)
    for load in loads[:split_at]:
        load.wait()
    film = jnp.dot(fourier, affine[...], preferred_element_type=jnp.float32)[:1]
    film_scale, film_shift = film[:, :channels], film[:, channels:]

    entries = float(cells * group_width * n)
    center, factor = moments(0, entries)
    scale = factor * gain_ref[0:1]
    offset = bias_ref[0:1]

    def active(values):
        return silu((values - center) * scale + offset).astype(jnp.bfloat16)

    for r in range(2):
        store_row(r + 1, active(features_ref[0, r].astype(jnp.float32)))
    halo_rows(0, halo1, active)

    first_conv = convolve(w1) + conv_bias_ref[0:1]
    first[...] = first_conv
    edges[...] = first_conv.astype(jnp.bfloat16).reshape(2, breadth, channels)
    stats[1, 0] = tile_of(
        jnp.sum(first_conv, axis=0, keepdims=True),
        jnp.sum(first_conv * first_conv, axis=0, keepdims=True),
    )
    share_stats(1)

    def edge_row(r):
        return edges.at[r]

    halo(1, edge_row, halo2, lambda copy: copy.start())
    for load in loads[split_at:split_too]:
        load.wait()
    center1, factor1 = moments(1, entries)
    scale1 = factor1 * gain_ref[1:2]
    offset1 = bias_ref[1:2]

    def middle(values):
        normed = (values - center1) * scale1 + offset1
        return silu(normed * (1.0 + film_scale) + film_shift).astype(jnp.bfloat16)

    for r in range(2):
        store_row(r + 1, middle(first[r * breadth : (r + 1) * breadth]))
    halo_rows(1, halo2, middle)

    second = convolve(w2) + conv_bias_ref[1:2]
    source = features_ref[0].astype(jnp.float32).reshape(cells, channels)
    level_one = ((source + second) * skip_gain).astype(jnp.bfloat16)
    cell = lax.rem(lax.broadcasted_iota(jnp.int32, (tokens, cells), 1), breadth)
    token = lax.broadcasted_iota(jnp.int32, (tokens, cells), 0)
    blocks = jnp.where(cell // 2 == token, 1.0, 0.0).astype(jnp.bfloat16)
    pooled = jnp.dot(blocks, level_one, preferred_element_type=jnp.float32) * 0.25
    pooled_ref[...] = pooled
    stats[2, 0] = tile_of(
        jnp.sum(pooled, axis=0, keepdims=True), jnp.sum(pooled * pooled, axis=0, keepdims=True)
    )
    share_stats(2)

    plane, side, core = me // 4, lax.rem(me // 2, 2), lax.rem(me, 2)
    gath[me] = pooled.astype(jnp.bfloat16)

    def shard(p, s, c):
        return p * 4 + s * 2 + c

    def pass_on(k, way):
        target = (me + 4, me - 4, shard(plane, 1 - side, core), shard(plane, side, 1 - core))[way]
        return remote(gath.at[k], gath.at[k], g_send.at[way, k], g_recv.at[k], target)

    def arrival(k):
        pltpu.make_async_copy(gath.at[k], gath.at[k], g_recv.at[k]).wait()

    def own_band(act):
        @pl.when(plane < planes - 1)
        def _():
            act(pass_on(me, 0))

        @pl.when(plane > 0)
        def _():
            act(pass_on(me, 1))

        act(pass_on(me, 2))
        act(pass_on(me, 3))

    own_band(lambda copy: copy.start())

    def spot(s):
        distance = (s + 1) // 2
        below = lax.rem(s, 2)
        p = plane + distance * (1 - 2 * below)
        valid = (p >= 0) & (p < planes)
        return p, below, valid

    def relay(s, act, waits):
        p, below, valid = spot(s)
        k = shard(p, side, core)

        @pl.when(valid & (s > 0))
        def _():
            if waits:
                arrival(k)

            @pl.when((below == 1) & (plane < planes - 1))
            def _():
                act(pass_on(k, 0))

            @pl.when((below == 0) & (plane > 0))
            def _():
                act(pass_on(k, 1))

            act(pass_on(k, 2))
            act(pass_on(k, 3))

    steps = 2 * planes - 1
    if steps > 1:
        relay(1, lambda copy: copy.start(), True)
        relay(2, lambda copy: copy.start(), True)

    for load in loads[split_too:]:
        load.wait()
    center2, factor2 = moments(2, float(tokens * group_width * n))
    scale2 = factor2 * gain_ref[2:3]
    offset2 = bias_ref[2:3]

    def normed(values):
        return ((values - center2) * scale2 + offset2).astype(jnp.bfloat16)

    wide = 4 * HEAD_DIM
    halves = channels // wide
    head_lane = lax.broadcasted_iota(jnp.int32, (tokens, wide), 1) // HEAD_DIM
    queries = jnp.dot(
        normed(pooled_ref[...]), wqkv[:, :channels], preferred_element_type=jnp.float32
    ).astype(jnp.bfloat16).astype(jnp.float32) * HEAD_DIM ** (-0.5)
    for g in range(halves):
        part = queries[:, g * wide : (g + 1) * wide]
        for i in range(4):
            qm[g, i * tokens : (i + 1) * tokens] = jnp.where(head_lane == i, part, 0.0).astype(
                jnp.bfloat16
            )
    top[...] = jnp.full(top.shape, -1e30, jnp.float32)
    total[...] = jnp.zeros(total.shape, jnp.float32)
    acc[...] = jnp.zeros(acc.shape, jnp.float32)

    def attend(s, carry):
        @pl.when(s + 2 < steps)
        def _():
            @pl.when(s > 0)
            def _():
                relay(s + 2, lambda copy: copy.start(), True)

        p, below, valid = spot(s)

        @pl.when(valid)
        def _():
            across = shard(p, 1 - side, core)
            arrival(across)
            pass_on(across, 3).start()
            arrival(shard(p, side, 1 - core))
            arrival(shard(p, 1 - side, 1 - core))
            rows = gath[pl.ds(p * 4, 4)].astype(jnp.float32).reshape(4 * tokens, channels)
            pairs = jnp.dot(
                normed(rows), wqkv[:, channels:], preferred_element_type=jnp.float32
            ).astype(jnp.bfloat16)
            for g in range(halves):
                keys = pairs[:, g * wide : (g + 1) * wide]
                values = pairs[:, channels + g * wide : channels + (g + 1) * wide]
                scores = lax.dot_general(
                    qm[g], keys, (((1,), (1,)), ((), ())), preferred_element_type=jnp.float32
                )
                old = top[g]
                rising = jnp.maximum(old, jnp.max(scores, axis=1, keepdims=True))
                fading = jnp.exp(old - rising)
                weights = jnp.exp(scores - rising)
                top[g] = rising
                total[g] = total[g] * fading + jnp.sum(weights, axis=1, keepdims=True)
                acc[g] = acc[g] * fading + jnp.dot(
                    weights.astype(jnp.bfloat16), values, preferred_element_type=jnp.float32
                )

        return carry

    lax.fori_loop(0, steps, attend, 0)

    attended = []
    for g in range(halves):
        mixed = acc[g] / total[g]
        part = jnp.zeros((tokens, wide), jnp.float32)
        for i in range(4):
            part = jnp.where(head_lane == i, mixed[i * tokens : (i + 1) * tokens], part)
        attended.append(part.astype(jnp.bfloat16))
    projected = jnp.dot(
        jnp.concatenate(attended, axis=1), wproj[...], preferred_element_type=jnp.float32
    )
    out_ref[0, 0] = ((pooled_ref[...] + projected + proj_bias_ref[...]) * skip_gain).astype(
        jnp.bfloat16
    )

    for phase in range(3):
        wait_stats(phase, stat_send)
    halo(0, feature_row, halo1, lambda copy: copy.wait_send())
    halo(1, edge_row, halo2, lambda copy: copy.wait_send())
    own_band(lambda copy: copy.wait_send())

    def settle(s, carry):
        relay(s, lambda copy: copy.wait_send(), False)
        p, below, valid = spot(s)

        @pl.when(valid)
        def _():
            pass_on(shard(p, 1 - side, core), 3).wait_send()

        return carry

    lax.fori_loop(0, steps, settle, 0)


def solution(mesh):
    n = mesh.shape["lat"]

    def local(
        features,
        noise_index,
        sigma_table,
        affine_weight,
        norm_gain,
        norm_bias,
        conv1_weight,
        conv2_weight,
        conv_bias,
        qkv_weight,
        proj_weight,
        proj_bias,
    ):
        breadth, channels = features.shape[2], features.shape[3]
        tokens = breadth // 2
        wide = 4 * HEAD_DIM
        halves = channels // wide
        bf16, f32 = jnp.bfloat16, jnp.float32
        smem = pl.BlockSpec(memory_space=pltpu.SMEM)
        vmem = pl.BlockSpec(memory_space=pltpu.VMEM)
        hbm = pl.BlockSpec(memory_space=pl.ANY)
        dma = pltpu.SemaphoreType.DMA

        def run(*refs):
            kernel(n, *refs)

        return pl.pallas_call(
            run,
            out_shape=jax.ShapeDtypeStruct((1, 1, tokens, channels), bf16),
            in_specs=[smem, smem, vmem, hbm, vmem, vmem, hbm, hbm, vmem, hbm, hbm, vmem],
            out_specs=vmem,
            scratch_shapes=[
                pltpu.VMEM(affine_weight.shape, bf16),
                pltpu.VMEM((3, 3 * channels, channels), bf16),
                pltpu.VMEM((3, 3 * channels, channels), bf16),
                pltpu.VMEM(qkv_weight.shape, bf16),
                pltpu.VMEM(proj_weight.shape, bf16),
                pltpu.VMEM((2, breadth, 3 * channels), bf16),
                pltpu.VMEM((2 * breadth, channels), f32),
                pltpu.VMEM((2, breadth, channels), bf16),
                pltpu.VMEM((2, breadth, channels), bf16),
                pltpu.VMEM((2, breadth, channels), bf16),
                pltpu.VMEM((3, n, 2 * channels // LANES, LANES), f32),
                pltpu.VMEM((n, tokens, channels), bf16),
                pltpu.VMEM((tokens, channels), f32),
                pltpu.VMEM((halves, 4 * tokens, wide), bf16),
                pltpu.VMEM((halves, 4 * tokens, 1), f32),
                pltpu.VMEM((halves, 4 * tokens, 1), f32),
                pltpu.VMEM((halves, 4 * tokens, wide), f32),
                dma((21,)),
                dma((3,)),
                dma((3,)),
                dma((2, 2)),
                dma((2, 2)),
                dma((4, n)),
                dma((n,)),
            ],
            compiler_params=pltpu.CompilerParams(
                collective_id=0, has_side_effects=True, vmem_limit_bytes=52 * 1024 * 1024
            ),
        )(
            noise_index,
            sigma_table,
            features,
            affine_weight,
            norm_gain,
            norm_bias,
            conv1_weight,
            conv2_weight,
            conv_bias,
            qkv_weight,
            proj_weight,
            proj_bias.reshape(1, channels),
        )

    return jax.shard_map(
        local,
        mesh=mesh,
        in_specs=(P("grp", "lat", None, None), P("grp")) + (P(),) * 10,
        out_specs=P("grp", "lat", None, None),
        check_vma=False,
    )
```

time: 250 us -> 55.3 us (0.22)
  blocking collectives: 99.9 us -> 0 us
  waiting for transfers between devices: 78.6 us -> 0 us
  Pallas kernels: 0 us -> 47.1 us
  local copies, waits for them, and re-layouts: 27.8 us -> 7.04 us
  between operations: 15.2 us -> 0.68 us
  matrix products: 12.7 us -> 0 us
  other arithmetic: 9.37 us -> 0 us
  starting transfers between devices: 5.41 us -> 0 us
    psum x3 -> x0, blocking collectives: 99.9 us -> none  [band_moments(): totals, squares = lax.psum((column_sums, column_squares), 'lat')]
    all_gather x2 -> x0, waiting for transfers between devices: 77 us -> none  [the longest x1 40.9 us: local(): lax.all_gather(projected[:, :, :, 1], 'lat', axis=1, tiled=True)]
    pallas_call x0 -> x1, Pallas kernels: none -> 47.1 us  [local(): pl.pallas_call(run, out_shape=jax.ShapeDtypeStruct((1, 1, tokens, channel...]
    dynamic_slice x6 -> x0, local copies, waits for them, and re-layouts: 9.6 us -> none  [the longest x4 8.14 us: key_span_step(): lax.dynamic_slice_in_dim(value_all, step_index * span_rows, span_rows, 1)]
    conv_general_dilated x2 -> x0, matrix products: 6.59 us -> none  [convolve(): lax.conv_general_dilated(values, kernel, (1, 1), ((0, 0), (1, 1)), dimens...]
    dot_general x7 -> x0, matrix products: 6.1 us -> none  [the longest x1 1.98 us: local(): jnp.dot(attended, proj_weight, preferred_element_type=jnp.float32)]
    ppermute x4 -> x0, starting transfers between devices: 5.37 us -> none  [the longest x2 2.76 us: with_halo(): lax.ppermute(lax.slice_in_dim(block, 0, width, axis=dim), axis, backward)]
    another operation x4 -> x0, local copies, waits for them, and re-layouts: 5.28 us -> none
  transfers between devices with their start and end apart: 6 -> 0, of which waited for: 3 -> 0; matrix products, arithmetic and copies ran while one was open for 2% -> 0% of each run, Pallas kernels for 0% -> 0%
where the time goes in v1:
time: 55.3 us; the launch traced here: 54.8 us
  Pallas kernels  47.1 us (85%)
  local copies, waits for them, and re-layouts  7.04 us (13%)
  between operations  0.68 us (1%)
    pallas_call x1, Pallas kernels, local(): pl.pallas_call(run, out_shape=jax.ShapeDtypeStruct((1, 1, tokens, channel...  47.1 us
    unnamed x17, local copies, waits for them, and re-layouts  7.04 us

profile of v1, /device:TPU:0, one launch (start us, length us, event | category | flops | bytes accessed | tf_op | source)
XLA Modules:
  0.0 54.8 jit_solution(16066417263804795933)
XLA Ops:
  0.7 0.0 copy-start
  0.7 1.0 %copy-done = bf16[512,512]{1,0:T(8,128)(2,1)S(1)} copy-done((bf16[512,512]{1,0:T(8,128)(2,1)S(1)}, bf16[512,512]{1,0:T(8,128)(2,1)}, u32[]{:S(2)}) %copy-start) | copy-done | bytes 524312
  1.7 0.0 copy-start.1
  1.7 1.0 %copy-done.1 = bf16[1,2,192,512]{3,2,1,0:T(8,128)(2,1)S(1)} copy-done((bf16[1,2,192,512]{3,2,1,0:T(8,128)(2,1)S(1)}, bf16[1,2,192,512]{3,2,1,0:T(8,128)(2,1)}, u32[]{:S(2)}) %copy-start.1) | copy-done | bytes 393240
  2.7 0.0 copy-start.2
  2.7 0.9 %copy-done.2 = bf16[128,1024]{1,0:T(8,128)(2,1)S(1)} copy-done((bf16[128,1024]{1,0:T(8,128)(2,1)S(1)}, bf16[128,1024]{1,0:T(8,128)(2,1)}, u32[]{:S(2)}) %copy-start.2) | copy-done | bytes 262168
  3.6 0.0 copy-start.3
  3.6 0.7 %copy-done.3 = f32[3,512]{1,0:T(4,128)S(1)} copy-done((f32[3,512]{1,0:T(4,128)S(1)}, f32[3,512]{1,0:T(4,128)}, u32[]{:S(2)}) %copy-start.3) | copy-done | bytes 6168
  4.3 0.0 copy-start.4
  4.3 0.7 %copy-done.4 = f32[3,512]{1,0:T(4,128)S(1)} copy-done((f32[3,512]{1,0:T(4,128)S(1)}, f32[3,512]{1,0:T(4,128)}, u32[]{:S(2)}) %copy-start.4) | copy-done | bytes 6168
  5.0 0.0 copy-start.5
  5.0 0.7 %copy-done.5 = f32[2,512]{1,0:T(2,128)S(1)} copy-done((f32[2,512]{1,0:T(2,128)S(1)}, f32[2,512]{1,0:T(2,128)}, u32[]{:S(2)}) %copy-start.5) | copy-done | bytes 4120
  5.7 0.0 copy-start.6
  5.7 0.7 %copy-done.6 = f32[512]{0:T(512)S(1)} copy-done((f32[512]{0:T(512)S(1)}, f32[512]{0:T(512)}, u32[]{:S(2)}) %copy-start.6) | copy-done | bytes 2072
  6.4 0.0 copy-start.7
  6.4 0.7 %copy-done.7 = f32[18]{0:T(128)S(1)} copy-done((f32[18]{0:T(128)S(1)}, f32[18]{0:T(128)}, u32[]{:S(2)}) %copy-start.7) | copy-done | bytes 96
  7.1 47.1 %shard_map.118 = bf16[1,1,96,512]{3,2,1,0:T(8,128)(2,1)S(1)} custom-call(s32[1]{0:T(128)S(6)} %copy.14.refs_0_, f32[18]{0:T(128)S(1)} %copy-done.7, bf16[1,2,192,512]{3,2,1,0:T(8,128)(2,1)S(1)} %copy-done.1, bf16[128,1024]{1,0:T(8,128)(2,1)S(1)} %copy-done.2, f32[3,512]{1,0:T(4,128)S(1)} %copy-done.3, f32[3,512]{1,0:T(4,128)S(1)} %copy-done.4, ...), custom_call_target="tpu_custom_call" | custom-call | tf_op jit(solution)/shard_map/pallas_call | solution.py:462
  54.1 0.6 %copy.15 = bf16[1,1,96,512]{3,2,1,0:T(8,128)(2,1)} copy(bf16[1,1,96,512]{3,2,1,0:T(8,128)(2,1)S(1)} %shard_map.118) | data formatting | bytes 196608
Async XLA Ops:
  0.7 1.0 %copy-start = (bf16[512,512]{1,0:T(8,128)(2,1)S(1)}, bf16[512,512]{1,0:T(8,128)(2,1)}, u32[]{:S(2)}) copy-start(bf16[512,512]{1,0:T(8,128)(2,1)} %refs_10_.1) | copy-start | bytes 1572868
  1.7 1.0 %copy-start.1 = (bf16[1,2,192,512]{3,2,1,0:T(8,128)(2,1)S(1)}, bf16[1,2,192,512]{3,2,1,0:T(8,128)(2,1)}, u32[]{:S(2)}) copy-start(bf16[1,2,192,512]{3,2,1,0:T(8,128)(2,1)} %refs_2_.1) | copy-start | bytes 1179652
  2.7 0.9 %copy-start.2 = (bf16[128,1024]{1,0:T(8,128)(2,1)S(1)}, bf16[128,1024]{1,0:T(8,128)(2,1)}, u32[]{:S(2)}) copy-start(bf16[128,1024]{1,0:T(8,128)(2,1)} %refs_3_.1) | copy-start | bytes 786436
  3.6 0.7 %copy-start.3 = (f32[3,512]{1,0:T(4,128)S(1)}, f32[3,512]{1,0:T(4,128)}, u32[]{:S(2)}) copy-start(f32[3,512]{1,0:T(4,128)} %refs_4_.1) | copy-start | bytes 18436
  4.3 0.7 %copy-start.4 = (f32[3,512]{1,0:T(4,128)S(1)}, f32[3,512]{1,0:T(4,128)}, u32[]{:S(2)}) copy-start(f32[3,512]{1,0:T(4,128)} %refs_5_.1) | copy-start | bytes 18436
  5.0 0.7 %copy-start.5 = (f32[2,512]{1,0:T(2,128)S(1)}, f32[2,512]{1,0:T(2,128)}, u32[]{:S(2)}) copy-start(f32[2,512]{1,0:T(2,128)} %refs_8_.1) | copy-start | bytes 12292
  5.7 0.7 %copy-start.6 = (f32[512]{0:T(512)S(1)}, f32[512]{0:T(512)}, u32[]{:S(2)}) copy-start(f32[512]{0:T(512)} %param.23) | copy-start | bytes 6148
  6.4 0.7 %copy-start.7 = (f32[18]{0:T(128)S(1)}, f32[18]{0:T(128)}, u32[]{:S(2)}) copy-start(f32[18]{0:T(128)} %refs_1_.1) | copy-start | bytes 220

commit v2 on v1

--- a/solution.py
+++ b/solution.py
@@ -33,19 +33,26 @@
 
 def kernel(
     n,
+    noise_hbm,
+    sigma_hbm,
+    features_hbm,
+    affine_hbm,
+    gain_hbm,
+    bias_hbm,
+    conv1_hbm,
+    conv2_hbm,
+    conv_bias_hbm,
+    qkv_hbm,
+    proj_hbm,
+    proj_bias_hbm,
+    out_ref,
     noise_ref,
     sigma_ref,
     features_ref,
-    affine_hbm,
     gain_ref,
     bias_ref,
-    conv1_hbm,
-    conv2_hbm,
     conv_bias_ref,
-    qkv_hbm,
-    proj_hbm,
     proj_bias_ref,
-    out_ref,
     affine,
     w1,
     w2,
@@ -79,7 +86,15 @@
     group_width = channels // GROUPS
     planes = n // 4
 
-    loads = []
+    loads = [
+        (features_hbm, features_ref),
+        (noise_hbm, noise_ref),
+        (sigma_hbm, sigma_ref),
+        (gain_hbm, gain_ref),
+        (bias_hbm, bias_ref),
+        (conv_bias_hbm, conv_bias_ref),
+        (proj_bias_hbm, proj_bias_ref),
+    ]
     for a in range(3):
         for b in range(3):
             loads.append((conv1_hbm.at[a, b], w1.at[b, pl.ds(a * channels, channels)]))
@@ -189,15 +204,31 @@
             def _():
                 store_row(k, jnp.zeros((breadth, channels), jnp.bfloat16))
 
-    def convolve(weights):
-        lhs = abuf[...].reshape(cells, 3 * channels)
-        column = lax.rem(lax.broadcasted_iota(jnp.int32, (cells, channels), 0), breadth)
-        low = jnp.dot(lhs, weights[0], preferred_element_type=jnp.float32)
-        result = jnp.where(column == 0, 0.0, pltpu.roll(low, 1, 0))
-        high = jnp.dot(lhs, weights[2], preferred_element_type=jnp.float32)
-        result += jnp.where(column == breadth - 1, 0.0, pltpu.roll(high, cells - 1, 0))
-        return result + jnp.dot(lhs, weights[1], preferred_element_type=jnp.float32)
-
+    def taps(lhs, weights, a, depth):
+        rows = lhs.shape[0]
+        column = lax.rem(lax.broadcasted_iota(jnp.int32, (rows, channels), 0), breadth)
+        part = [
+            jnp.dot(
+                lhs,
+                weights[b, a * channels : (a + depth) * channels],
+                preferred_element_type=jnp.float32,
+            )
+            for b in range(3)
+        ]
+        low = jnp.where(column == 0, 0.0, pltpu.roll(part[0], 1, 0))
+        high = jnp.where(column == breadth - 1, 0.0, pltpu.roll(part[2], rows - 1, 0))
+        return low + high + part[1]
+
+    def convolve_own(weights):
+        for r in range(2):
+            lhs = abuf[r, :, (1 - r) * channels : (3 - r) * channels]
+            first[r * breadth : (r + 1) * breadth] = taps(lhs, weights, 1 - r, 2)
+
+    def convolve_rest(weights, r):
+        lhs = abuf[r, :, 2 * r * channels : (2 * r + 1) * channels]
+        return first[r * breadth : (r + 1) * breadth] + taps(lhs, weights, 2 * r, 1)
+
+    loads[0].wait()
     source = features_ref[0].astype(jnp.float32).reshape(cells, channels)
     stats[0, 0] = tile_of(
         jnp.sum(source, axis=0, keepdims=True), jnp.sum(source * source, axis=0, keepdims=True)
@@ -210,13 +241,13 @@
 
     halo(0, feature_row, halo1, lambda copy: copy.start())
 
+    for load in loads[1:split_at]:
+        load.wait()
     sigma = jnp.full((8, 2 * FREQS), sigma_ref[noise_ref[0]], jnp.float32)
     lane = lax.broadcasted_iota(jnp.int32, (8, 2 * FREQS), 1)
     order = lax.rem(lane, FREQS).astype(jnp.float32)
     angles = (jnp.log(sigma) / 4.0) * jnp.exp(-math.log(10000.0) * order / FREQS)
     fourier = jnp.where(lane < FREQS, jnp.cos(angles), jnp.sin(angles)).astype(jnp.bfloat16)
-    for load in loads[:split_at]:
-        load.wait()
     film = jnp.dot(fourier, affine[...], preferred_element_type=jnp.float32)[:1]
     film_scale, film_shift = film[:, :channels], film[:, channels:]
 
@@ -230,9 +261,12 @@
 
     for r in range(2):
         store_row(r + 1, active(features_ref[0, r].astype(jnp.float32)))
+    convolve_own(w1)
     halo_rows(0, halo1, active)
 
-    first_conv = convolve(w1) + conv_bias_ref[0:1]
+    first_conv = (
+        jnp.concatenate([convolve_rest(w1, r) for r in range(2)], axis=0) + conv_bias_ref[0:1]
+    )
     first[...] = first_conv
     edges[...] = first_conv.astype(jnp.bfloat16).reshape(2, breadth, channels)
     stats[1, 0] = tile_of(
@@ -257,9 +291,12 @@
 
     for r in range(2):
         store_row(r + 1, middle(first[r * breadth : (r + 1) * breadth]))
+    convolve_own(w2)
     halo_rows(1, halo2, middle)
 
-    second = convolve(w2) + conv_bias_ref[1:2]
+    second = (
+        jnp.concatenate([convolve_rest(w2, r) for r in range(2)], axis=0) + conv_bias_ref[1:2]
+    )
     source = features_ref[0].astype(jnp.float32).reshape(cells, channels)
     level_one = ((source + second) * skip_gain).astype(jnp.bfloat16)
     cell = lax.rem(lax.broadcasted_iota(jnp.int32, (tokens, cells), 1), breadth)
@@ -278,24 +315,31 @@
     def shard(p, s, c):
         return p * 4 + s * 2 + c
 
-    def pass_on(k, way):
+    pieces = 2 if tokens % 32 == 0 else 1
+    piece = tokens // pieces
+
+    def pass_on(k, way, h):
         target = (me + 4, me - 4, shard(plane, 1 - side, core), shard(plane, side, 1 - core))[way]
-        return remote(gath.at[k], gath.at[k], g_send.at[way, k], g_recv.at[k], target)
-
-    def arrival(k):
-        pltpu.make_async_copy(gath.at[k], gath.at[k], g_recv.at[k]).wait()
+        band = gath.at[k, pl.ds(h * piece, piece)]
+        return remote(band, band, g_send.at[way, k, h], g_recv.at[k, h], target)
+
+    def arrival(k, h):
+        band = gath.at[k, pl.ds(h * piece, piece)]
+        pltpu.make_async_copy(band, band, g_recv.at[k, h]).wait()
 
     def own_band(act):
-        @pl.when(plane < planes - 1)
-        def _():
-            act(pass_on(me, 0))
-
-        @pl.when(plane > 0)
-        def _():
-            act(pass_on(me, 1))
-
-        act(pass_on(me, 2))
-        act(pass_on(me, 3))
+        for h in range(pieces):
+
+            @pl.when(plane < planes - 1)
+            def _():
+                act(pass_on(me, 0, h))
+
+            @pl.when(plane > 0)
+            def _():
+                act(pass_on(me, 1, h))
+
+            act(pass_on(me, 2, h))
+            act(pass_on(me, 3, h))
 
     own_band(lambda copy: copy.start())
 
@@ -312,19 +356,20 @@
 
         @pl.when(valid & (s > 0))
         def _():
-            if waits:
-                arrival(k)
-
-            @pl.when((below == 1) & (plane < planes - 1))
-            def _():
-                act(pass_on(k, 0))
-
-            @pl.when((below == 0) & (plane > 0))
-            def _():
-                act(pass_on(k, 1))
-
-            act(pass_on(k, 2))
-            act(pass_on(k, 3))
+            for h in range(pieces):
+                if waits:
+                    arrival(k, h)
+
+                @pl.when((below == 1) & (plane < planes - 1))
+                def _():
+                    act(pass_on(k, 0, h))
+
+                @pl.when((below == 0) & (plane > 0))
+                def _():
+                    act(pass_on(k, 1, h))
+
+                act(pass_on(k, 2, h))
+                act(pass_on(k, 3, h))
 
     steps = 2 * planes - 1
     if steps > 1:
@@ -368,10 +413,12 @@
         @pl.when(valid)
         def _():
             across = shard(p, 1 - side, core)
-            arrival(across)
-            pass_on(across, 3).start()
-            arrival(shard(p, side, 1 - core))
-            arrival(shard(p, 1 - side, 1 - core))
+            for h in range(pieces):
+                arrival(across, h)
+                pass_on(across, 3, h).start()
+            for h in range(pieces):
+                arrival(shard(p, side, 1 - core), h)
+                arrival(shard(p, 1 - side, 1 - core), h)
             rows = gath[pl.ds(p * 4, 4)].astype(jnp.float32).reshape(4 * tokens, channels)
             pairs = jnp.dot(
                 normed(rows), wqkv[:, channels:], preferred_element_type=jnp.float32
@@ -422,7 +469,8 @@
 
         @pl.when(valid)
         def _():
-            pass_on(shard(p, 1 - side, core), 3).wait_send()
+            for h in range(pieces):
+                pass_on(shard(p, 1 - side, core), 3, h).wait_send()
 
         return carry
 
@@ -451,9 +499,8 @@
         wide = 4 * HEAD_DIM
         halves = channels // wide
         bf16, f32 = jnp.bfloat16, jnp.float32
-        smem = pl.BlockSpec(memory_space=pltpu.SMEM)
         vmem = pl.BlockSpec(memory_space=pltpu.VMEM)
-        hbm = pl.BlockSpec(memory_space=pl.ANY)
+        hbm = pl.BlockSpec(memory_space=pltpu.HBM)
         dma = pltpu.SemaphoreType.DMA
 
         def run(*refs):
@@ -462,9 +509,16 @@
         return pl.pallas_call(
             run,
             out_shape=jax.ShapeDtypeStruct((1, 1, tokens, channels), bf16),
-            in_specs=[smem, smem, vmem, hbm, vmem, vmem, hbm, hbm, vmem, hbm, hbm, vmem],
+            in_specs=[hbm] * 12,
             out_specs=vmem,
             scratch_shapes=[
+                pltpu.SMEM(noise_index.shape, jnp.int32),
+                pltpu.SMEM(sigma_table.shape, f32),
+                pltpu.VMEM(features.shape, bf16),
+                pltpu.VMEM(norm_gain.shape, f32),
+                pltpu.VMEM(norm_bias.shape, f32),
+                pltpu.VMEM(conv_bias.shape, f32),
+                pltpu.VMEM((1, channels), f32),
                 pltpu.VMEM(affine_weight.shape, bf16),
                 pltpu.VMEM((3, 3 * channels, channels), bf16),
                 pltpu.VMEM((3, 3 * channels, channels), bf16),
@@ -482,16 +536,16 @@
                 pltpu.VMEM((halves, 4 * tokens, 1), f32),
                 pltpu.VMEM((halves, 4 * tokens, 1), f32),
                 pltpu.VMEM((halves, 4 * tokens, wide), f32),
-                dma((21,)),
+                dma((28,)),
                 dma((3,)),
                 dma((3,)),
                 dma((2, 2)),
                 dma((2, 2)),
-                dma((4, n)),
-                dma((n,)),
+                dma((4, n, 2)),
+                dma((n, 2)),
             ],
             compiler_params=pltpu.CompilerParams(
-                collective_id=0, has_side_effects=True, vmem_limit_bytes=52 * 1024 * 1024
+                collective_id=0, has_side_effects=True, vmem_limit_bytes=64 * 1024 * 1024
             ),
         )(
             noise_index,

time: 55.3 us -> 48.3 us (0.87)
  local copies, waits for them, and re-layouts: 7.04 us -> 1.54 us
  Pallas kernels: 47.1 us -> 46 us
    unnamed x17 -> x1, local copies, waits for them, and re-layouts: 7.04 us -> 1.54 us
    pallas_call x1, Pallas kernels: 47.1 us -> 46 us  [local(): pl.pallas_call(run, out_shape=jax.ShapeDtypeStruct((1, 1, tokens, channel...]
where the time goes in v2:
time: 48.3 us; the launch traced here: 48.2 us
  Pallas kernels  46 us (95%)
  local copies, waits for them, and re-layouts  1.54 us (3%)
  between operations  0.66 us (1%)
    pallas_call x1, Pallas kernels, local(): pl.pallas_call(run, out_shape=jax.ShapeDtypeStruct((1, 1, tokens, channel...  46 us
    unnamed x1, local copies, waits for them, and re-layouts  1.54 us

profile of v2, /device:TPU:0, one launch (start us, length us, event | category | flops | bytes accessed | tf_op | source)
XLA Modules:
  0.0 48.2 jit_solution(11626095399649210887)
XLA Ops:
  0.7 46.0 %shard_map.118 = bf16[1,1,96,512]{3,2,1,0:T(8,128)(2,1)} custom-call(s32[1]{0:T(128)S(6)} %copy.14.refs_0_, f32[18]{0:T(128)} %refs_1_.1, bf16[1,2,192,512]{3,2,1,0:T(8,128)(2,1)} %refs_2_.1, bf16[128,1024]{1,0:T(8,128)(2,1)} %refs_3_.1, f32[3,512]{1,0:T(4,128)} %refs_4_.1, f32[3,512]{1,0:T(4,128)} %refs_5_.1, bf16[3,3,512,512]{3,2,1,0:T(8,128)(2,1)} %refs_6_.1, ...), custom_call_target="tpu_custom_call" | custom-call | tf_op jit(solution)/shard_map/pallas_call | solution.py:509
  46.6 1.5 %copy.15 = bf16[1,1,96,512]{3,2,1,0:T(8,128)(2,1)} copy(bf16[1,1,96,512]{3,2,1,0:T(8,128)(2,1)} %shard_map.118) | data formatting | bytes 196608

commit v3 on v2

--- a/solution.py
+++ b/solution.py
@@ -121,7 +121,7 @@
         )
         return carry
 
-    lax.fori_loop(1, n, greet, 0)
+    lax.fori_loop(1, n, greet, 0, unroll=n <= 16)
 
     def remote(src, dst, send, recv, target):
         return pltpu.make_async_remote_copy(
@@ -149,7 +149,7 @@
             ).start()
             return carry
 
-        lax.fori_loop(1, n, share, 0)
+        lax.fori_loop(1, n, share, 0, unroll=n <= 16)
 
     def wait_stats(phase, sem):
         others = stats.at[phase, pl.ds(1, n - 1)]
@@ -401,12 +401,16 @@
     total[...] = jnp.zeros(total.shape, jnp.float32)
     acc[...] = jnp.zeros(acc.shape, jnp.float32)
 
+    if steps > 3:
+        relay(3, lambda copy: copy.start(), True)
+        relay(4, lambda copy: copy.start(), True)
+
     def attend(s, carry):
-        @pl.when(s + 2 < steps)
+        @pl.when(s + 4 < steps)
         def _():
             @pl.when(s > 0)
             def _():
-                relay(s + 2, lambda copy: copy.start(), True)
+                relay(s + 4, lambda copy: copy.start(), True)
 
         p, below, valid = spot(s)
 

time: 48.3 us -> 47.4 us (0.981)
  Pallas kernels: 46 us -> 45 us
    pallas_call x1, Pallas kernels: 46 us -> 45 us  [local(): pl.pallas_call(run, out_shape=jax.ShapeDtypeStruct((1, 1, tokens, channel...]
where the time goes in v3:
time: 47.4 us; the launch traced here: 47.2 us
  Pallas kernels  45 us (95%)
  local copies, waits for them, and re-layouts  1.54 us (3%)
  between operations  0.66 us (1%)
    pallas_call x1, Pallas kernels, local(): pl.pallas_call(run, out_shape=jax.ShapeDtypeStruct((1, 1, tokens, channel...  45 us
    unnamed x1, local copies, waits for them, and re-layouts  1.54 us

profile of v3, /device:TPU:0, one launch (start us, length us, event | category | flops | bytes accessed | tf_op | source)
XLA Modules:
  0.0 47.2 jit_solution(16398947701016073877)
XLA Ops:
  0.7 45.0 %shard_map.118 = bf16[1,1,96,512]{3,2,1,0:T(8,128)(2,1)} custom-call(s32[1]{0:T(128)S(6)} %copy.14.refs_0_, f32[18]{0:T(128)} %refs_1_.1, bf16[1,2,192,512]{3,2,1,0:T(8,128)(2,1)} %refs_2_.1, bf16[128,1024]{1,0:T(8,128)(2,1)} %refs_3_.1, f32[3,512]{1,0:T(4,128)} %refs_4_.1, f32[3,512]{1,0:T(4,128)} %refs_5_.1, bf16[3,3,512,512]{3,2,1,0:T(8,128)(2,1)} %refs_6_.1, ...), custom_call_target="tpu_custom_call" | custom-call | tf_op jit(solution)/shard_map/pallas_call | solution.py:513
  45.7 1.5 %copy.15 = bf16[1,1,96,512]{3,2,1,0:T(8,128)(2,1)} copy(bf16[1,1,96,512]{3,2,1,0:T(8,128)(2,1)} %shard_map.118) | data formatting | bytes 196608
